TPU v7x, 256 devices: a whole 4x4x8 slice. The times are simulated.
256 devices in a mesh: seq: 32 (over y, z), tp: 8 (over x, core).
Axes of the slice: x: 4, y: 4, z: 8, core: 2. Of those that a mesh axis runs over, the one named last changes fastest.
Arguments:
- decode_query: bfloat16 [4, 8192], P(None, 'tp'), may hold values from -180 to 180, as said below
- cache_keys: bfloat16 [4, 65536, 1024], P(None, 'seq', 'tp'), may hold values from -6 to 6
- cache_values: bfloat16 [4, 65536, 1024], P(None, 'seq', 'tp'), may hold values from -6 to 6
- cache_len: int32 [4], replicated, may hold values from 2048 to 65536, as said below
- prefill_rows: bfloat16 [1024, 8192], P(None, 'seq'), may hold values from -8 to 8
- key_weight: bfloat16 [8192, 1024], P('seq', 'tp'), may hold values from -0.0625 to 0.0625
- value_weight: bfloat16 [8192, 1024], P('seq', 'tp'), may hold values from -0.0625 to 0.0625
- span_request: int32 [1024], replicated, may hold values from 0 to 3
- span_target: int32 [1024, 1], replicated, may hold values from 0 to 31; in each aligned block of 32 rows (0 to 31, 32 to 63, ...) at most 2 rows name the same one
- out_weight: bfloat16 [8192, 8192], P('tp', 'seq'), may hold values from -0.1875 to 0.1875
Outputs:
- layer_out: bfloat16 [4, 8192], P(None, 'seq')
- appended_keys: bfloat16 [2048, 1024], P('seq', 'tp')
- appended_values: bfloat16 [2048, 1024], P('seq', 'tp')
Inputs may be any that keep to these rules, and one draw needn't show every extreme that they name: `cache_len`: some request has all 65536 positions live. `decode_query`: in the hidden draw some queries are large multiples of cached keys. `span_target`: among the 32 tokens owned by one index of seq, at most 2 share a target, and 2 do in some owners.
All inputs are finite; a program needn't handle non-finite values.
Results may differ from a plain program's by a relative error of at most 0.03.
Values may be sent and summed in bfloat16 or wider, within the bound.
No kernel may reach another device: no remote copies, remote signals or barrier semaphores. Data moves between devices by JAX's collectives and lax.ppermute only.
A program may use at most 64 MiB of HBM per device.

v0:
```python
import functools

import jax
import jax.numpy as jnp
from jax import lax
from jax.experimental import pallas as pl
from jax.experimental.pallas import tpu as pltpu
from jax.sharding import PartitionSpec as P

H = 64
KVH = 8
HD = 128
CAP = 2
DEAD = -(2.0**100)
NY = 4
NZ = 8
Y_STEPS = (1, 3, 2)
TAIL = 8
VMEM = pltpu.VMEM
SMEM = pltpu.SMEM
MIB = 1 << 20


def whole(space=VMEM):
    return pl.BlockSpec(memory_space=space)


def in_hbm(array):
    return pltpu.with_memory_space_constraint(array, pltpu.HBM)


def project_kernel(
    rows_hbm, key_hbm, value_hbm, own_ref, to1_ref, to2_ref, to3_ref, rows_ref, weight_ref, sems
):
    copies = [
        pltpu.make_async_copy(key_hbm, weight_ref.at[:, :HD], sems.at[0]),
        pltpu.make_async_copy(value_hbm, weight_ref.at[:, HD:], sems.at[1]),
        pltpu.make_async_copy(rows_hbm, rows_ref, sems.at[2]),
    ]
    for copy in copies:
        copy.start()
    for copy in copies:
        copy.wait()
    weight = weight_ref[...]
    y = lax.axis_index("seq") // NZ
    size = own_ref.shape[0]
    for k, ref in zip((0,) + Y_STEPS, (own_ref, to1_ref, to2_ref, to3_ref)):
        first = pl.multiple_of(lax.rem(y + k, NY) * size, size)
        ref[...] = jnp.dot(
            rows_ref[pl.ds(first, size), :], weight, preferred_element_type=jnp.float32
        ).astype(jnp.bfloat16)


def project(rows, key_weight, value_weight):
    tokens, features = rows.shape
    return pl.pallas_call(
        project_kernel,
        in_specs=[whole(pltpu.HBM)] * 3,
        out_specs=[whole()] * NY,
        out_shape=[jax.ShapeDtypeStruct((tokens // NY, 2 * HD), jnp.bfloat16)] * NY,
        scratch_shapes=[
            VMEM((tokens, features), jnp.bfloat16),
            VMEM((features, 2 * HD), jnp.bfloat16),
            pltpu.SemaphoreType.DMA((3,)),
        ],
        compiler_params=pltpu.CompilerParams(vmem_limit_bytes=8 * MIB),
        name="project",
    )(in_hbm(rows), in_hbm(key_weight), in_hbm(value_weight))


def fold_kernel(after_ref, own_ref, from1_ref, from2_ref, from3_ref, out_ref):
    total = own_ref[...].astype(jnp.float32)
    for ref in (from1_ref, from2_ref, from3_ref):
        total = total + ref[...].astype(jnp.float32)
    total = total.astype(jnp.bfloat16)
    size = total.shape[0] // NZ
    for z in range(NZ):
        place = (NZ - 1 - z) * size
        out_ref[place : place + size, :] = total[z * size : (z + 1) * size]


def fold(after, parts):
    return pl.pallas_call(
        fold_kernel,
        in_specs=[whole()] * 5,
        out_specs=whole(),
        out_shape=jax.ShapeDtypeStruct(parts[0].shape, jnp.bfloat16),
        compiler_params=pltpu.CompilerParams(vmem_limit_bytes=8 * MIB),
        name="fold",
    )(after, *parts)


def stacked_queries(query_ref, per_group):
    query = query_ref[...]
    return jnp.concatenate(
        [query[:, h * HD : (h + 1) * HD] for h in range(per_group)], axis=0
    )


def cache_kernel(
    requests,
    per_group,
    len_hbm,
    query_hbm,
    target_hbm,
    request_hbm,
    keys_hbm,
    values_hbm,
    o_ref,
    m_ref,
    l_ref,
    place_key_ref,
    place_value_ref,
    live_ref,
    stacked_ref,
    len_ref,
    query_ref,
    target_ref,
    request_ref,
    keys_ref,
    values_ref,
    query_rows,
    o_rows,
    m_rows,
    l_rows,
    small_sems,
    sems,
):
    seq_index = lax.axis_index("seq")
    rows = requests * per_group
    local_len = keys_ref.shape[1]
    tokens = live_ref.shape[1]
    small = [
        pltpu.make_async_copy(source, dest, small_sems.at[i])
        for i, (source, dest) in enumerate(
            (
                (len_hbm, len_ref),
                (query_hbm, query_ref),
                (target_hbm, target_ref),
                (request_hbm, request_ref),
            )
        )
    ]
    key_copies = [
        pltpu.make_async_copy(keys_hbm.at[r], keys_ref.at[r], sems.at[0, r])
        for r in range(requests)
    ]
    value_copies = [
        pltpu.make_async_copy(values_hbm.at[r], values_ref.at[r], sems.at[1, r])
        for r in range(requests)
    ]
    for copy in small:
        copy.start()
    for r in range(requests):
        key_copies[r].start()
        value_copies[r].start()
    for copy in small:
        copy.wait()

    per_tile = HD // tokens
    first = pl.multiple_of(seq_index // per_tile * HD, HD)
    shift = lax.rem(HD - lax.rem(seq_index, per_tile) * tokens, HD)

    def own(ref):
        tile = jnp.broadcast_to(ref[:, pl.ds(first, HD)], (8, HD))
        return pltpu.roll(tile, shift, 1)[0:1, :tokens]

    target_row = own(target_ref)
    target = jnp.broadcast_to(target_row, (tokens, tokens))
    i = lax.broadcasted_iota(jnp.int32, (tokens, tokens), 0)
    j = lax.broadcasted_iota(jnp.int32, (tokens, tokens), 1)
    column = jnp.sum(jnp.where(i == j, target, 0), axis=1, keepdims=True)
    rank = jnp.sum(jnp.where((column == target) & (i < j), 1, 0), axis=0, keepdims=True)
    slot = target_row * CAP + rank
    count = place_key_ref.shape[0]
    row = lax.broadcasted_iota(jnp.int32, (count, tokens), 0)
    dest, within = count // TAIL - 1 - row // TAIL, row % TAIL
    wanted = jnp.broadcast_to(slot, (count, tokens))
    is_key = (within < CAP) & (wanted == dest * CAP + within)
    is_value = (within >= CAP) & (within < 2 * CAP) & (wanted == dest * CAP + within - CAP)
    place_key_ref[...] = jnp.where(is_key, 1.0, 0.0).astype(jnp.bfloat16)
    place_value_ref[...] = jnp.where(is_value, 1.0, 0.0).astype(jnp.bfloat16)
    owner = jnp.broadcast_to(own(request_ref), (rows, tokens))
    mine = lax.broadcasted_iota(jnp.int32, (rows, tokens), 0) % requests
    live_ref[...] = jnp.where(owner == mine, 1.0, 0.0)

    stacked = stacked_queries(query_ref, per_group)
    stacked_ref[...] = stacked
    query_rows[...] = stacked.astype(jnp.float32)
    for r in range(requests):
        query = query_rows[pl.ds(r, per_group, stride=requests), :].astype(jnp.bfloat16)
        key_copies[r].wait()
        scores = lax.dot_general(
            query, keys_ref[r], (((1,), (1,)), ((), ())), preferred_element_type=jnp.float32
        ) * HD ** (-0.5)
        position = seq_index * local_len + lax.broadcasted_iota(jnp.int32, scores.shape, 1)
        allowed = position < len_ref[r]
        scores = jnp.where(allowed, scores, DEAD)
        top = jnp.max(scores, axis=1, keepdims=True)
        weights = jnp.where(allowed, jnp.exp(scores - top), 0.0)
        own_rows = pl.ds(r * per_group, per_group)
        l_rows[own_rows, :] = jnp.broadcast_to(
            jnp.sum(weights, axis=1, keepdims=True), (per_group, HD)
        )
        m_rows[own_rows, :] = jnp.broadcast_to(top, (per_group, HD))
        value_copies[r].wait()
        o_rows[own_rows, :] = jnp.dot(
            weights.astype(jnp.bfloat16), values_ref[r], preferred_element_type=jnp.float32
        )
    for h in range(per_group):
        to = pl.ds(h * requests, requests)
        of = pl.ds(h, requests, stride=per_group)
        o_ref[to, :] = o_rows[of, :]
        m_ref[to, :] = m_rows[of, :]
        l_ref[to, :] = l_rows[of, :]


def cache_part(cache_len, query, keys, values, target, request_ids, seq_count):
    requests, local_len, _ = keys.shape
    per_group = query.shape[1] // HD
    rows = requests * per_group
    tokens = target.shape[1] // seq_count
    f32 = jnp.float32
    table = jax.ShapeDtypeStruct((rows, HD), f32)
    place = jax.ShapeDtypeStruct((seq_count * TAIL, tokens), jnp.bfloat16)
    operands = (cache_len, query, target, request_ids, keys, values)
    return pl.pallas_call(
        functools.partial(cache_kernel, requests, per_group),
        in_specs=[whole(pltpu.HBM)] * 6,
        out_specs=[whole()] * 7,
        out_shape=[
            table,
            table,
            table,
            place,
            place,
            jax.ShapeDtypeStruct((rows, tokens), f32),
            jax.ShapeDtypeStruct((rows, HD), query.dtype),
        ],
        scratch_shapes=[SMEM(cache_len.shape, cache_len.dtype)]
        + [VMEM(a.shape, a.dtype) for a in operands[1:]]
        + [VMEM((rows, HD), f32)] * 4
        + [pltpu.SemaphoreType.DMA((4,)), pltpu.SemaphoreType.DMA((2, requests))],
        cost_estimate=pl.CostEstimate(
            flops=4 * rows * local_len * HD,
            bytes_accessed=4 * requests * local_len * HD,
            transcendentals=rows * local_len,
        ),
        compiler_params=pltpu.CompilerParams(vmem_limit_bytes=16 * MIB),
        name="cache_part",
    )(*[in_hbm(a) for a in operands])


def span_kernel(
    parts_ref,
    o_ref,
    m_ref,
    l_ref,
    place_key_ref,
    place_value_ref,
    live_ref,
    query_ref,
    out_ref,
):
    rows = o_ref.shape[0]
    seq_count = out_ref.shape[0]
    total = parts_ref[0].astype(jnp.float32)
    for source in range(1, parts_ref.shape[0]):
        total = total + parts_ref[source].astype(jnp.float32)
    owned = total.astype(jnp.bfloat16)
    span_k, span_v = owned[:, :HD], owned[:, HD:]
    live = live_ref[...] > 0.5
    scores = lax.dot_general(
        query_ref[...], span_k, (((1,), (1,)), ((), ())), preferred_element_type=jnp.float32
    ) * HD ** (-0.5)
    scores = jnp.where(live, scores, DEAD)
    m_cache = m_ref[:, 0:1]
    reference = (
        jnp.maximum(m_cache, jnp.max(scores, axis=1, keepdims=True))
        .astype(jnp.bfloat16)
        .astype(jnp.float32)
    )
    weights = jnp.where(live, jnp.exp(scores - reference), 0.0)
    scale = jnp.exp(m_cache - reference)
    row_sum = scale * l_ref[:, 0:1] + jnp.sum(weights, axis=1, keepdims=True)
    weighted = scale * o_ref[...] + jnp.dot(
        weights.astype(jnp.bfloat16), span_v, preferred_element_type=jnp.float32
    )
    empty = row_sum == 0.0
    shared = jnp.where(empty, 0.0, weighted / jnp.where(empty, 1.0, row_sum)).astype(jnp.bfloat16)
    sum_high = row_sum.astype(jnp.bfloat16).astype(jnp.float32)
    sum_low = row_sum - sum_high
    lane = lax.broadcasted_iota(jnp.int32, (rows, HD), 1)
    row = lax.broadcasted_iota(jnp.int32, (rows, HD), 0)
    spread = jnp.where(lane == row, reference, 0.0)
    spread = jnp.where(lane == row + rows, sum_high, spread)
    spread = jnp.where(lane == row + 2 * rows, sum_low, spread)
    stats = jnp.sum(spread, axis=0, keepdims=True)
    tail = jnp.dot(place_key_ref[...], span_k, preferred_element_type=jnp.float32)
    tail = tail + jnp.dot(place_value_ref[...], span_v, preferred_element_type=jnp.float32)
    within = lax.broadcasted_iota(jnp.int32, tail.shape, 0) % TAIL
    tail = jnp.where(within == 2 * CAP, jnp.broadcast_to(stats, tail.shape), tail)
    out_ref[:, rows:, :] = tail.astype(jnp.bfloat16).reshape(seq_count, TAIL, HD)
    for dest in range(seq_count):
        out_ref[dest, :rows, :] = shared


def span_part(parts, cache_state, seq_count):
    rows = cache_state[0].shape[0]
    return pl.pallas_call(
        span_kernel,
        in_specs=[whole()] * (1 + len(cache_state)),
        out_specs=whole(),
        out_shape=jax.ShapeDtypeStruct((seq_count, rows + TAIL, HD), jnp.bfloat16),
        compiler_params=pltpu.CompilerParams(vmem_limit_bytes=8 * MIB),
        name="span_part",
    )(parts, *cache_state)


def out_kernel(requests, message_ref, weight_ref, out_ref):
    seq_count = message_ref.shape[0]
    rows = message_ref.shape[1] - TAIL
    per_group = rows // requests
    tails = message_ref[:, rows:, :].astype(jnp.float32)
    within = lax.broadcasted_iota(jnp.int32, tails.shape, 1)
    stats = jnp.sum(jnp.where(within == 2 * CAP, tails, 0.0), axis=1)
    m = stats[:, :rows]
    sums = stats[:, rows : 2 * rows] + stats[:, 2 * rows : 3 * rows]
    share = jnp.exp(m - jnp.max(m, axis=0, keepdims=True)) * sums
    share = share / jnp.sum(share, axis=0, keepdims=True)
    share = share.T
    total = jnp.zeros((rows, HD), jnp.float32)
    for source in range(seq_count):
        total = total + share[:, source : source + 1] * message_ref[source, :rows, :].astype(
            jnp.float32
        )
    attended = jnp.concatenate(
        [total[h * requests : (h + 1) * requests] for h in range(per_group)], axis=1
    ).astype(jnp.bfloat16)
    projected = jnp.dot(attended, weight_ref[...], preferred_element_type=jnp.float32)
    for dest in range(out_ref.shape[0]):
        out_ref[dest] = projected


def out_part(messages, out_weight, requests, tp_count):
    return pl.pallas_call(
        functools.partial(out_kernel, requests),
        in_specs=[whole()] * 2,
        out_specs=whole(),
        out_shape=jax.ShapeDtypeStruct((tp_count, requests, out_weight.shape[1]), jnp.float32),
        compiler_params=pltpu.CompilerParams(vmem_limit_bytes=8 * MIB),
        name="out_part",
    )(messages, out_weight)


def finish_kernel(
    message_ref, share_ref, out_hbm, key_hbm, value_hbm, out_ref, key_ref, value_ref, sems
):
    rows = message_ref.shape[1] - TAIL
    tails = message_ref[:, rows:, :]
    count = tails.shape[0]
    tails = jnp.concatenate([tails[p : p + 1] for p in reversed(range(count))], axis=0)
    key_ref[...] = tails[:, :CAP].reshape(key_ref.shape)
    value_ref[...] = tails[:, CAP : 2 * CAP].reshape(value_ref.shape)
    copies = [
        pltpu.make_async_copy(source, dest, sems.at[i])
        for i, (source, dest) in enumerate(
            ((out_ref, out_hbm), (key_ref, key_hbm), (value_ref, value_hbm))
        )
    ]
    copies[1].start()
    copies[2].start()
    out_ref[...] = jnp.sum(share_ref[...], axis=0).astype(jnp.bfloat16)
    copies[0].start()
    for copy in copies:
        copy.wait()


def finish(messages, shares):
    slots = jax.ShapeDtypeStruct((messages.shape[0] * CAP, HD), jnp.bfloat16)
    outs = [jax.ShapeDtypeStruct(shares.shape[1:], jnp.bfloat16), slots, slots]
    return pl.pallas_call(
        finish_kernel,
        in_specs=[whole()] * 2,
        out_specs=[whole(pltpu.HBM)] * 3,
        out_shape=outs,
        scratch_shapes=[VMEM(a.shape, a.dtype) for a in outs] + [pltpu.SemaphoreType.DMA((3,))],
        compiler_params=pltpu.CompilerParams(vmem_limit_bytes=8 * MIB),
        name="finish",
    )(messages, shares)


def per_device(
    decode_query,
    cache_keys,
    cache_values,
    cache_len,
    prefill_rows,
    key_weight,
    value_weight,
    span_request,
    span_target,
    out_weight,
):
    seq_count = lax.axis_size("seq")
    tp_count = lax.axis_size("tp")
    requests = cache_keys.shape[0]
    rows = requests * decode_query.shape[1] // HD
    pre_dev = prefill_rows.shape[0] // seq_count

    own, *sent = project(prefill_rows, key_weight, value_weight)
    seq = [(y, z) for y in range(NY) for z in range(NZ)]
    came = [
        lax.ppermute(part, "seq", [(y * NZ + z, (y + k) % NY * NZ + z) for y, z in seq])
        for k, part in zip(Y_STEPS, sent)
    ]
    targets = span_target.T
    request_ids = span_request.reshape(targets.shape)
    cache_state = cache_part(
        cache_len, decode_query, cache_keys, cache_values, targets, request_ids, seq_count
    )
    partial = fold(cache_state[0], [own, *came]).reshape(NZ, pre_dev, 2 * HD)
    parts = lax.all_to_all(
        partial,
        "seq",
        split_axis=0,
        concat_axis=0,
        tiled=True,
        axis_index_groups=[[y * NZ + z for z in reversed(range(NZ))] for y in range(NY)],
    )
    outgoing = span_part(parts, cache_state, seq_count)
    messages = lax.all_to_all(
        outgoing,
        "seq",
        split_axis=0,
        concat_axis=0,
        tiled=True,
        axis_index_groups=[list(reversed(range(seq_count)))],
    )
    shares = out_part(messages, out_weight, requests, tp_count)
    shares = lax.all_to_all(
        shares,
        "tp",
        split_axis=0,
        concat_axis=0,
        tiled=True,
        axis_index_groups=[list(reversed(range(tp_count)))],
    )
    return finish(messages, shares)


def solution(mesh):
    placed = (
        P(None, "tp"),
        P(None, "seq", "tp"),
        P(None, "seq", "tp"),
        P(),
        P(None, "seq"),
        P("seq", "tp"),
        P("seq", "tp"),
        P(),
        P(),
        P("tp", "seq"),
    )
    return jax.shard_map(
        per_device,
        mesh=mesh,
        in_specs=placed,
        out_specs=(P(None, "seq"), P("seq", "tp"), P("seq", "tp")),
        check_vma=False,
    )
```

profile of v0, /device:TPU:1, one launch (start us, length us, event | category | flops | bytes accessed | tf_op | source)
XLA Modules:
  0.0 54.4 jit_solution(10360511431182032862)
XLA Ops:
  0.6 1.4 %project.1 = (bf16[256,256]{1,0:T(8,128)(2,1)S(1)}, bf16[256,256]{1,0:T(8,128)(2,1)S(1)}, bf16[256,256]{1,0:T(8,128)(2,1)S(1)}, bf16[256,256]{1,0:T(8,128)(2,1)S(1)}) custom-call(bf16[1024,256]{1,0:T(8,128)(2,1)} %rows_hbm.1, bf16[256,128]{1,0:T(8,128)(2,1)} %key_hbm.1, bf16[256,128]{1,0:T(8,128)(2,1)} %value_hbm.1), custom_call_target="tpu_custom_call" | custom-call | tf_op jit(solution)/shard_map/project/pallas_call | solution.py:56
  2.1 2.2 %collective-permute-start = (bf16[256,256]{1,0:T(8,128)(2,1)S(1)}, bf16[256,256]{1,0:T(8,128)(2,1)S(1)}, u32[]{:S(2)}, u32[]{:S(2)}) collective-permute-start(bf16[256,256]{1,0:T(8,128)(2,1)S(1)} %get-tuple-element.16), channel_id=1, source_target_pairs={{0,64},{8,72},{16,80},{24,88},{32,96},{40,104},{48,112},{56,120},{... | collective-permute-start | bytes 393224 | tf_op jit(solution)/shard_map/ppermute | solution.py:414
  4.3 1.5 %collective-permute-start.1 = (bf16[256,256]{1,0:T(8,128)(2,1)S(1)}, bf16[256,256]{1,0:T(8,128)(2,1)S(1)}, u32[]{:S(2)}, u32[]{:S(2)}) collective-permute-start(bf16[256,256]{1,0:T(8,128)(2,1)S(1)} %get-tuple-element.17), channel_id=1, source_target_pairs={{0,192},{8,200},{16,208},{24,216},{32,224},{40,232},{48,240},{56,2... | collective-permute-start | bytes 393224 | tf_op jit(solution)/shard_map/ppermute | solution.py:414
  5.8 1.6 %collective-permute-start.2 = (bf16[256,256]{1,0:T(8,128)(2,1)S(1)}, bf16[256,256]{1,0:T(8,128)(2,1)S(1)}, u32[]{:S(2)}, u32[]{:S(2)}) collective-permute-start(bf16[256,256]{1,0:T(8,128)(2,1)S(1)} %get-tuple-element.18), channel_id=1, source_target_pairs={{0,128},{8,136},{16,144},{24,152},{32,160},{40,168},{48,176},{56,1... | collective-permute-start | bytes 393224 | tf_op jit(solution)/shard_map/ppermute | solution.py:414
  7.4 4.7 %cache_part.1 = (f32[32,128]{1,0:T(8,128)S(1)}, f32[32,128]{1,0:T(8,128)S(1)}, f32[32,128]{1,0:T(8,128)S(1)}, bf16[256,32]{1,0:T(8,128)(2,1)S(1)}, bf16[256,32]{...) custom-call(s32[4]{0:T(128)} %len_hbm.1, bf16[4,1024]{1,0:T(4,128)(2,1)} %query_hbm.1, ...), custom_call_target="tpu_custom_call" | custom-call | flops 33554432 | bytes 4194304 | tf_op jit(solution)/shard_map/cache_part/pallas_call | solution.py:227
  12.1 0.0 copy-start
  12.1 0.0 collective-permute-done.from1_ref
  12.1 0.0 collective-permute-done.1.from2_ref
  12.1 0.0 collective-permute-done.2.from3_ref
  12.1 0.1 fold.1
  12.2 13.9 %all_to_all.15.parts_ref = bf16[8,32,256]{2,1,0:T(8,128)(2,1)S(1)} all-to-all(bf16[8,32,256]{2,1,0:T(8,128)(2,1)S(1)} %bitcast.3), channel_id=1, replica_groups={{56,48,40,32,24,16,8,0},{120,112,104,96,88,80,72,64},{184,176,168,160,1..., dimensions={0} | all-to-all | bytes 262144 | tf_op jit(solution)/shard_map/all_to_all | solution.py:423
  26.1 0.5 span_part.1
  26.6 14.7 %all_to_all.16.message_ref = bf16[32,40,128]{2,1,0:T(8,128)(2,1)S(1)} all-to-all(bf16[32,40,128]{2,1,0:T(8,128)(2,1)S(1)} %span_part.1), channel_id=1, replica_groups={{248,240,232,224,216,208,200,192,184,176,168,160,152,144,136,128,120,11..., dimensions={0} | all-to-all | bytes 655360 | tf_op jit(solution)/shard_map/all_to_all | solution.py:432
  41.3 0.0 copy-done
  41.3 0.7 %out_part.1 = f32[8,4,256]{2,1,0:T(4,128)S(1)} custom-call(bf16[32,40,128]{2,1,0:T(8,128)(2,1)S(1)} %all_to_all.16.message_ref, bf16[1024,256]{1,0:T(8,128)(2,1)S(1)} %copy-done), custom_call_target="tpu_custom_call" | custom-call | tf_op jit(solution)/shard_map/out_part/pallas_call | solution.py:346
  41.9 11.8 %all_to_all.17.share_ref = f32[8,4,256]{2,1,0:T(4,128)S(1)} all-to-all(f32[8,4,256]{2,1,0:T(4,128)S(1)} %out_part.1), channel_id=1, replica_groups={{7,6,5,4,3,2,1,0},{15,14,13,12,11,10,9,8},{23,22,21,20,19,18,17,16},{31..., dimensions={0} | all-to-all | bytes 65536 | tf_op jit(solution)/shard_map/all_to_all | solution.py:441
  53.7 0.7 %finish.1 = (bf16[4,256]{1,0:T(4,128)(2,1)}, bf16[64,128]{1,0:T(8,128)(2,1)}, bf16[64,128]{1,0:T(8,128)(2,1)}) custom-call(bf16[32,40,128]{2,1,0:T(8,128)(2,1)S(1)} %all_to_all.16.message_ref, f32[8,4,256]{2,1,0:T(4,128)S(1)} %all_to_all.17.share_ref), custom_call_target="tpu_custom_call" | custom-call | tf_op jit(solution)/shard_map/finish/pallas_call | solution.py:382
Async XLA Ops:
  2.1 10.0 %collective-permute-start = (bf16[256,256]{1,0:T(8,128)(2,1)S(1)}, bf16[256,256]{1,0:T(8,128)(2,1)S(1)}, u32[]{:S(2)}, u32[]{:S(2)}) collective-permute-start(bf16[256,256]{1,0:T(8,128)(2,1)S(1)} %get-tuple-element.16), channel_id=1, source_target_pairs={{0,64},{8,72},{16,80},{24,88},{32,96},{40,104},{48,112},{56,120},{... | collective-permute-start | bytes 393224 | tf_op jit(solution)/shard_map/ppermute | solution.py:414
  4.3 7.8 %collective-permute-start.1 = (bf16[256,256]{1,0:T(8,128)(2,1)S(1)}, bf16[256,256]{1,0:T(8,128)(2,1)S(1)}, u32[]{:S(2)}, u32[]{:S(2)}) collective-permute-start(bf16[256,256]{1,0:T(8,128)(2,1)S(1)} %get-tuple-element.17), channel_id=1, source_target_pairs={{0,192},{8,200},{16,208},{24,216},{32,224},{40,232},{48,240},{56,2... | collective-permute-start | bytes 393224 | tf_op jit(solution)/shard_map/ppermute | solution.py:414
  5.8 6.3 %collective-permute-start.2 = (bf16[256,256]{1,0:T(8,128)(2,1)S(1)}, bf16[256,256]{1,0:T(8,128)(2,1)S(1)}, u32[]{:S(2)}, u32[]{:S(2)}) collective-permute-start(bf16[256,256]{1,0:T(8,128)(2,1)S(1)} %get-tuple-element.18), channel_id=1, source_target_pairs={{0,128},{8,136},{16,144},{24,152},{32,160},{40,168},{48,176},{56,1... | collective-permute-start | bytes 393224 | tf_op jit(solution)/shard_map/ppermute | solution.py:414
  12.1 29.2 %copy-start = (bf16[1024,256]{1,0:T(8,128)(2,1)S(1)}, bf16[1024,256]{1,0:T(8,128)(2,1)}, u32[]{:S(2)}) copy-start(bf16[1024,256]{1,0:T(8,128)(2,1)} %weight_ref.1) | copy-start | bytes 1572868
where the time goes:
time: 54.6 us; the launch traced here: 54.4 us
  blocking collectives  40.3 us (74%)
  Pallas kernels  8.02 us (15%)
  starting transfers between devices  5.29 us (10%)
  between operations  0.69 us (1%)
    all_to_all x1, blocking collectives, per_device(): lax.all_to_all(outgoing, 'seq', split_axis=0, concat_axis=0, tiled=True,...  14.7 us
    all_to_all x1, blocking collectives, per_device(): lax.all_to_all(partial, 'seq', split_axis=0, concat_axis=0, tiled=True, a...  13.9 us
    all_to_all x1, blocking collectives, per_device(): lax.all_to_all(shares, 'tp', split_axis=0, concat_axis=0, tiled=True, axi...  11.8 us
    ppermute x3, starting transfers between devices, per_device(): lax.ppermute(part, 'seq', [(y * NZ + z, (y + k) % NY * NZ + z) for y, z i...  5.29 us
    pallas_call x1, Pallas kernels, cache_part(): pl.pallas_call(functools.partial(cache_kernel, requests, per_group), in_s...  4.67 us
    pallas_call x1, Pallas kernels, project(): pl.pallas_call(project_kernel, in_specs=[whole(pltpu.HBM)] * 3, out_specs...  1.45 us
  transfers between devices with their start and end apart: 3, of which 0 were waited for; matrix products, arithmetic and copies ran while one was open for 0% of the time, Pallas kernels for 9%

commit v1 on v0

--- a/solution.py
+++ b/solution.py
@@ -19,6 +19,12 @@
 VMEM = pltpu.VMEM
 SMEM = pltpu.SMEM
 MIB = 1 << 20
+
+
+def listed(place):
+    y = (place >> 3 & 1) * 2 + (place >> 4 & 1)
+    z = (place & 1) * 4 + (place >> 1 & 1) * 2 + (place >> 2 & 1)
+    return NY * NZ - 1 - (y * NZ + z)
 
 
 def whole(space=VMEM):
@@ -174,7 +180,7 @@
     slot = target_row * CAP + rank
     count = place_key_ref.shape[0]
     row = lax.broadcasted_iota(jnp.int32, (count, tokens), 0)
-    dest, within = count // TAIL - 1 - row // TAIL, row % TAIL
+    dest, within = listed(row // TAIL), row % TAIL
     wanted = jnp.broadcast_to(slot, (count, tokens))
     is_key = (within < CAP) & (wanted == dest * CAP + within)
     is_value = (within >= CAP) & (within < 2 * CAP) & (wanted == dest * CAP + within - CAP)
@@ -359,7 +365,9 @@
     rows = message_ref.shape[1] - TAIL
     tails = message_ref[:, rows:, :]
     count = tails.shape[0]
-    tails = jnp.concatenate([tails[p : p + 1] for p in reversed(range(count))], axis=0)
+    tails = jnp.concatenate(
+        [tails[p : p + 1] for p in (listed(seq) for seq in range(count))], axis=0
+    )
     key_ref[...] = tails[:, :CAP].reshape(key_ref.shape)
     value_ref[...] = tails[:, CAP : 2 * CAP].reshape(value_ref.shape)
     copies = [
@@ -435,7 +443,7 @@
         split_axis=0,
         concat_axis=0,
         tiled=True,
-        axis_index_groups=[list(reversed(range(seq_count)))],
+        axis_index_groups=[[listed(place) for place in range(seq_count)]],
     )
     shares = out_part(messages, out_weight, requests, tp_count)
     shares = lax.all_to_all(

time: 54.6 us -> 53.5 us (0.980)
  blocking collectives: 40.3 us -> 39.2 us
    all_to_all x1, blocking collectives: 14.7 us -> 12.8 us  [per_device(): lax.all_to_all(outgoing, 'seq', split_axis=0, concat_axis=0, tiled=True,...]
    all_to_all x1, blocking collectives: 11.8 us -> 12.5 us  [per_device(): lax.all_to_all(shares, 'tp', split_axis=0, concat_axis=0, tiled=True, axi...]
where the time goes in v1:
time: 53.5 us; the launch traced here: 53.3 us
  blocking collectives  39.2 us (73%)
  Pallas kernels  8.08 us (15%)
  starting transfers between devices  5.29 us (10%)
  between operations  0.7 us (1%)
    all_to_all x1, blocking collectives, per_device(): lax.all_to_all(partial, 'seq', split_axis=0, concat_axis=0, tiled=True, a...  13.9 us
    all_to_all x1, blocking collectives, per_device(): lax.all_to_all(outgoing, 'seq', split_axis=0, concat_axis=0, tiled=True,...  12.8 us
    all_to_all x1, blocking collectives, per_device(): lax.all_to_all(shares, 'tp', split_axis=0, concat_axis=0, tiled=True, axi...  12.5 us
    ppermute x3, starting transfers between devices, per_device(): lax.ppermute(part, 'seq', [(y * NZ + z, (y + k) % NY * NZ + z) for y, z i...  5.29 us
    pallas_call x1, Pallas kernels, cache_part(): pl.pallas_call(functools.partial(cache_kernel, requests, per_group), in_s...  4.73 us
    pallas_call x1, Pallas kernels, project(): pl.pallas_call(project_kernel, in_specs=[whole(pltpu.HBM)] * 3, out_specs...  1.45 us
  transfers between devices with their start and end apart: 3, of which 0 were waited for; matrix products, arithmetic and copies ran while one was open for 0% of the time, Pallas kernels for 9%

profile of v1, /device:TPU:1, one launch (start us, length us, event | category | flops | bytes accessed | tf_op | source)
XLA Modules:
  0.0 53.3 jit_solution(17340102790081991086)
XLA Ops:
  0.6 1.4 %project.1 = (bf16[256,256]{1,0:T(8,128)(2,1)S(1)}, bf16[256,256]{1,0:T(8,128)(2,1)S(1)}, bf16[256,256]{1,0:T(8,128)(2,1)S(1)}, bf16[256,256]{1,0:T(8,128)(2,1)S(1)}) custom-call(bf16[1024,256]{1,0:T(8,128)(2,1)} %rows_hbm.1, bf16[256,128]{1,0:T(8,128)(2,1)} %key_hbm.1, bf16[256,128]{1,0:T(8,128)(2,1)} %value_hbm.1), custom_call_target="tpu_custom_call" | custom-call | tf_op jit(solution)/shard_map/project/pallas_call | solution.py:62
  2.1 2.2 %collective-permute-start = (bf16[256,256]{1,0:T(8,128)(2,1)S(1)}, bf16[256,256]{1,0:T(8,128)(2,1)S(1)}, u32[]{:S(2)}, u32[]{:S(2)}) collective-permute-start(bf16[256,256]{1,0:T(8,128)(2,1)S(1)} %get-tuple-element.16), channel_id=1, source_target_pairs={{0,64},{8,72},{16,80},{24,88},{32,96},{40,104},{48,112},{56,120},{... | collective-permute-start | bytes 393224 | tf_op jit(solution)/shard_map/ppermute | solution.py:422
  4.3 1.5 %collective-permute-start.1 = (bf16[256,256]{1,0:T(8,128)(2,1)S(1)}, bf16[256,256]{1,0:T(8,128)(2,1)S(1)}, u32[]{:S(2)}, u32[]{:S(2)}) collective-permute-start(bf16[256,256]{1,0:T(8,128)(2,1)S(1)} %get-tuple-element.17), channel_id=1, source_target_pairs={{0,192},{8,200},{16,208},{24,216},{32,224},{40,232},{48,240},{56,2... | collective-permute-start | bytes 393224 | tf_op jit(solution)/shard_map/ppermute | solution.py:422
  5.8 1.6 %collective-permute-start.2 = (bf16[256,256]{1,0:T(8,128)(2,1)S(1)}, bf16[256,256]{1,0:T(8,128)(2,1)S(1)}, u32[]{:S(2)}, u32[]{:S(2)}) collective-permute-start(bf16[256,256]{1,0:T(8,128)(2,1)S(1)} %get-tuple-element.18), channel_id=1, source_target_pairs={{0,128},{8,136},{16,144},{24,152},{32,160},{40,168},{48,176},{56,1... | collective-permute-start | bytes 393224 | tf_op jit(solution)/shard_map/ppermute | solution.py:422
  7.4 4.7 %cache_part.1 = (f32[32,128]{1,0:T(8,128)S(1)}, f32[32,128]{1,0:T(8,128)S(1)}, f32[32,128]{1,0:T(8,128)S(1)}, bf16[256,32]{1,0:T(8,128)(2,1)S(1)}, bf16[256,32]{...) custom-call(s32[4]{0:T(128)} %len_hbm.1, bf16[4,1024]{1,0:T(4,128)(2,1)} %query_hbm.1, ...), custom_call_target="tpu_custom_call" | custom-call | flops 33554432 | bytes 4194304 | tf_op jit(solution)/shard_map/cache_part/pallas_call | solution.py:233
  12.1 0.0 copy-start
  12.1 0.0 collective-permute-done.from1_ref
  12.1 0.0 collective-permute-done.1.from2_ref
  12.1 0.0 collective-permute-done.2.from3_ref
  12.2 0.1 fold.1
  12.2 13.9 %all_to_all.15.parts_ref = bf16[8,32,256]{2,1,0:T(8,128)(2,1)S(1)} all-to-all(bf16[8,32,256]{2,1,0:T(8,128)(2,1)S(1)} %bitcast.3), channel_id=1, replica_groups={{56,48,40,32,24,16,8,0},{120,112,104,96,88,80,72,64},{184,176,168,160,1..., dimensions={0} | all-to-all | bytes 262144 | tf_op jit(solution)/shard_map/all_to_all | solution.py:431
  26.1 0.5 span_part.1
  26.6 12.8 %all_to_all.16.message_ref = bf16[32,40,128]{2,1,0:T(8,128)(2,1)S(1)} all-to-all(bf16[32,40,128]{2,1,0:T(8,128)(2,1)S(1)} %span_part.1), channel_id=1, replica_groups={{248,216,232,200,240,208,224,192,120,88,104,72,112,80,96,64,184,152,168..., dimensions={0} | all-to-all | bytes 655360 | tf_op jit(solution)/shard_map/all_to_all | solution.py:440
  39.4 0.0 copy-done
  39.4 0.7 %out_part.1 = f32[8,4,256]{2,1,0:T(4,128)S(1)} custom-call(bf16[32,40,128]{2,1,0:T(8,128)(2,1)S(1)} %all_to_all.16.message_ref, bf16[1024,256]{1,0:T(8,128)(2,1)S(1)} %copy-done), custom_call_target="tpu_custom_call" | custom-call | tf_op jit(solution)/shard_map/out_part/pallas_call | solution.py:352
  40.1 12.5 %all_to_all.17.share_ref = f32[8,4,256]{2,1,0:T(4,128)S(1)} all-to-all(f32[8,4,256]{2,1,0:T(4,128)S(1)} %out_part.1), channel_id=1, replica_groups={{7,6,5,4,3,2,1,0},{15,14,13,12,11,10,9,8},{23,22,21,20,19,18,17,16},{31..., dimensions={0} | all-to-all | bytes 65536 | tf_op jit(solution)/shard_map/all_to_all | solution.py:449
  52.6 0.7 %finish.1 = (bf16[4,256]{1,0:T(4,128)(2,1)}, bf16[64,128]{1,0:T(8,128)(2,1)}, bf16[64,128]{1,0:T(8,128)(2,1)}) custom-call(bf16[32,40,128]{2,1,0:T(8,128)(2,1)S(1)} %all_to_all.16.message_ref, f32[8,4,256]{2,1,0:T(4,128)S(1)} %all_to_all.17.share_ref), custom_call_target="tpu_custom_call" | custom-call | tf_op jit(solution)/shard_map/finish/pallas_call | solution.py:390
Async XLA Ops:
  2.1 10.0 %collective-permute-start = (bf16[256,256]{1,0:T(8,128)(2,1)S(1)}, bf16[256,256]{1,0:T(8,128)(2,1)S(1)}, u32[]{:S(2)}, u32[]{:S(2)}) collective-permute-start(bf16[256,256]{1,0:T(8,128)(2,1)S(1)} %get-tuple-element.16), channel_id=1, source_target_pairs={{0,64},{8,72},{16,80},{24,88},{32,96},{40,104},{48,112},{56,120},{... | collective-permute-start | bytes 393224 | tf_op jit(solution)/shard_map/ppermute | solution.py:422
  4.3 7.8 %collective-permute-start.1 = (bf16[256,256]{1,0:T(8,128)(2,1)S(1)}, bf16[256,256]{1,0:T(8,128)(2,1)S(1)}, u32[]{:S(2)}, u32[]{:S(2)}) collective-permute-start(bf16[256,256]{1,0:T(8,128)(2,1)S(1)} %get-tuple-element.17), channel_id=1, source_target_pairs={{0,192},{8,200},{16,208},{24,216},{32,224},{40,232},{48,240},{56,2... | collective-permute-start | bytes 393224 | tf_op jit(solution)/shard_map/ppermute | solution.py:422
  5.8 6.3 %collective-permute-start.2 = (bf16[256,256]{1,0:T(8,128)(2,1)S(1)}, bf16[256,256]{1,0:T(8,128)(2,1)S(1)}, u32[]{:S(2)}, u32[]{:S(2)}) collective-permute-start(bf16[256,256]{1,0:T(8,128)(2,1)S(1)} %get-tuple-element.18), channel_id=1, source_target_pairs={{0,128},{8,136},{16,144},{24,152},{32,160},{40,168},{48,176},{56,1... | collective-permute-start | bytes 393224 | tf_op jit(solution)/shard_map/ppermute | solution.py:422
  12.1 27.3 %copy-start = (bf16[1024,256]{1,0:T(8,128)(2,1)S(1)}, bf16[1024,256]{1,0:T(8,128)(2,1)}, u32[]{:S(2)}) copy-start(bf16[1024,256]{1,0:T(8,128)(2,1)} %weight_ref.1) | copy-start | bytes 1572868

commit v2 on v1

--- a/solution.py
+++ b/solution.py
@@ -81,7 +81,7 @@
     total = total.astype(jnp.bfloat16)
     size = total.shape[0] // NZ
     for z in range(NZ):
-        place = (NZ - 1 - z) * size
+        place = listed(NY * NZ - NZ + z) * size
         out_ref[place : place + size, :] = total[z * size : (z + 1) * size]
 
 
@@ -427,6 +427,7 @@
     cache_state = cache_part(
         cache_len, decode_query, cache_keys, cache_values, targets, request_ids, seq_count
     )
+    z_order = [listed(NY * NZ - NZ + place) for place in range(NZ)]
     partial = fold(cache_state[0], [own, *came]).reshape(NZ, pre_dev, 2 * HD)
     parts = lax.all_to_all(
         partial,
@@ -434,7 +435,7 @@
         split_axis=0,
         concat_axis=0,
         tiled=True,
-        axis_index_groups=[[y * NZ + z for z in reversed(range(NZ))] for y in range(NY)],
+        axis_index_groups=[[y * NZ + z for z in z_order] for y in range(NY)],
     )
     outgoing = span_part(parts, cache_state, seq_count)
     messages = lax.all_to_all(

time: 53.5 us -> 53.5 us (level)
  no operation moved by 1% of the time
where the time goes in v2:
time: 53.5 us; the launch traced here: 53.3 us
  blocking collectives  39.2 us (73%)
  Pallas kernels  8.08 us (15%)
  starting transfers between devices  5.29 us (10%)
  between operations  0.7 us (1%)
    all_to_all x1, blocking collectives, per_device(): lax.all_to_all(partial, 'seq', split_axis=0, concat_axis=0, tiled=True, a...  13.6 us
    all_to_all x1, blocking collectives, per_device(): lax.all_to_all(outgoing, 'seq', split_axis=0, concat_axis=0, tiled=True,...  13.1 us
    all_to_all x1, blocking collectives, per_device(): lax.all_to_all(shares, 'tp', split_axis=0, concat_axis=0, tiled=True, axi...  12.5 us
    ppermute x3, starting transfers between devices, per_device(): lax.ppermute(part, 'seq', [(y * NZ + z, (y + k) % NY * NZ + z) for y, z i...  5.29 us
    pallas_call x1, Pallas kernels, cache_part(): pl.pallas_call(functools.partial(cache_kernel, requests, per_group), in_s...  4.73 us
    pallas_call x1, Pallas kernels, project(): pl.pallas_call(project_kernel, in_specs=[whole(pltpu.HBM)] * 3, out_specs...  1.45 us
  transfers between devices with their start and end apart: 3, of which 0 were waited for; matrix products, arithmetic and copies ran while one was open for 0% of the time, Pallas kernels for 9%

profile of v2, /device:TPU:1, one launch (start us, length us, event | category | flops | bytes accessed | tf_op | source)
XLA Modules:
  0.0 53.3 jit_solution(9201965624141714873)
XLA Ops:
  0.6 1.4 %project.1 = (bf16[256,256]{1,0:T(8,128)(2,1)S(1)}, bf16[256,256]{1,0:T(8,128)(2,1)S(1)}, bf16[256,256]{1,0:T(8,128)(2,1)S(1)}, bf16[256,256]{1,0:T(8,128)(2,1)S(1)}) custom-call(bf16[1024,256]{1,0:T(8,128)(2,1)} %rows_hbm.1, bf16[256,128]{1,0:T(8,128)(2,1)} %key_hbm.1, bf16[256,128]{1,0:T(8,128)(2,1)} %value_hbm.1), custom_call_target="tpu_custom_call" | custom-call | tf_op jit(solution)/shard_map/project/pallas_call | solution.py:62
  2.1 2.2 %collective-permute-start = (bf16[256,256]{1,0:T(8,128)(2,1)S(1)}, bf16[256,256]{1,0:T(8,128)(2,1)S(1)}, u32[]{:S(2)}, u32[]{:S(2)}) collective-permute-start(bf16[256,256]{1,0:T(8,128)(2,1)S(1)} %get-tuple-element.16), channel_id=1, source_target_pairs={{0,64},{8,72},{16,80},{24,88},{32,96},{40,104},{48,112},{56,120},{... | collective-permute-start | bytes 393224 | tf_op jit(solution)/shard_map/ppermute | solution.py:422
  4.3 1.5 %collective-permute-start.1 = (bf16[256,256]{1,0:T(8,128)(2,1)S(1)}, bf16[256,256]{1,0:T(8,128)(2,1)S(1)}, u32[]{:S(2)}, u32[]{:S(2)}) collective-permute-start(bf16[256,256]{1,0:T(8,128)(2,1)S(1)} %get-tuple-element.17), channel_id=1, source_target_pairs={{0,192},{8,200},{16,208},{24,216},{32,224},{40,232},{48,240},{56,2... | collective-permute-start | bytes 393224 | tf_op jit(solution)/shard_map/ppermute | solution.py:422
  5.8 1.6 %collective-permute-start.2 = (bf16[256,256]{1,0:T(8,128)(2,1)S(1)}, bf16[256,256]{1,0:T(8,128)(2,1)S(1)}, u32[]{:S(2)}, u32[]{:S(2)}) collective-permute-start(bf16[256,256]{1,0:T(8,128)(2,1)S(1)} %get-tuple-element.18), channel_id=1, source_target_pairs={{0,128},{8,136},{16,144},{24,152},{32,160},{40,168},{48,176},{56,1... | collective-permute-start | bytes 393224 | tf_op jit(solution)/shard_map/ppermute | solution.py:422
  7.4 4.7 %cache_part.1 = (f32[32,128]{1,0:T(8,128)S(1)}, f32[32,128]{1,0:T(8,128)S(1)}, f32[32,128]{1,0:T(8,128)S(1)}, bf16[256,32]{1,0:T(8,128)(2,1)S(1)}, bf16[256,32]{...) custom-call(s32[4]{0:T(128)} %len_hbm.1, bf16[4,1024]{1,0:T(4,128)(2,1)} %query_hbm.1, ...), custom_call_target="tpu_custom_call" | custom-call | flops 33554432 | bytes 4194304 | tf_op jit(solution)/shard_map/cache_part/pallas_call | solution.py:233
  12.1 0.0 copy-start
  12.1 0.0 collective-permute-done.from1_ref
  12.1 0.0 collective-permute-done.1.from2_ref
  12.1 0.0 collective-permute-done.2.from3_ref
  12.2 0.1 fold.1
  12.2 13.6 %all_to_all.15.parts_ref = bf16[8,32,256]{2,1,0:T(8,128)(2,1)S(1)} all-to-all(bf16[8,32,256]{2,1,0:T(8,128)(2,1)S(1)} %bitcast.3), channel_id=1, replica_groups={{56,24,40,8,48,16,32,0},{120,88,104,72,112,80,96,64},{184,152,168,136,1..., dimensions={0} | all-to-all | bytes 262144 | tf_op jit(solution)/shard_map/all_to_all | solution.py:432
  25.8 0.5 span_part.1
  26.3 13.1 %all_to_all.16.message_ref = bf16[32,40,128]{2,1,0:T(8,128)(2,1)S(1)} all-to-all(bf16[32,40,128]{2,1,0:T(8,128)(2,1)S(1)} %span_part.1), channel_id=1, replica_groups={{248,216,232,200,240,208,224,192,120,88,104,72,112,80,96,64,184,152,168..., dimensions={0} | all-to-all | bytes 655360 | tf_op jit(solution)/shard_map/all_to_all | solution.py:441
  39.4 0.0 copy-done
  39.4 0.7 %out_part.1 = f32[8,4,256]{2,1,0:T(4,128)S(1)} custom-call(bf16[32,40,128]{2,1,0:T(8,128)(2,1)S(1)} %all_to_all.16.message_ref, bf16[1024,256]{1,0:T(8,128)(2,1)S(1)} %copy-done), custom_call_target="tpu_custom_call" | custom-call | tf_op jit(solution)/shard_map/out_part/pallas_call | solution.py:352
  40.1 12.5 %all_to_all.17.share_ref = f32[8,4,256]{2,1,0:T(4,128)S(1)} all-to-all(f32[8,4,256]{2,1,0:T(4,128)S(1)} %out_part.1), channel_id=1, replica_groups={{7,6,5,4,3,2,1,0},{15,14,13,12,11,10,9,8},{23,22,21,20,19,18,17,16},{31..., dimensions={0} | all-to-all | bytes 65536 | tf_op jit(solution)/shard_map/all_to_all | solution.py:450
  52.6 0.7 %finish.1 = (bf16[4,256]{1,0:T(4,128)(2,1)}, bf16[64,128]{1,0:T(8,128)(2,1)}, bf16[64,128]{1,0:T(8,128)(2,1)}) custom-call(bf16[32,40,128]{2,1,0:T(8,128)(2,1)S(1)} %all_to_all.16.message_ref, f32[8,4,256]{2,1,0:T(4,128)S(1)} %all_to_all.17.share_ref), custom_call_target="tpu_custom_call" | custom-call | tf_op jit(solution)/shard_map/finish/pallas_call | solution.py:390
Async XLA Ops:
  2.1 10.0 %collective-permute-start = (bf16[256,256]{1,0:T(8,128)(2,1)S(1)}, bf16[256,256]{1,0:T(8,128)(2,1)S(1)}, u32[]{:S(2)}, u32[]{:S(2)}) collective-permute-start(bf16[256,256]{1,0:T(8,128)(2,1)S(1)} %get-tuple-element.16), channel_id=1, source_target_pairs={{0,64},{8,72},{16,80},{24,88},{32,96},{40,104},{48,112},{56,120},{... | collective-permute-start | bytes 393224 | tf_op jit(solution)/shard_map/ppermute | solution.py:422
  4.3 7.8 %collective-permute-start.1 = (bf16[256,256]{1,0:T(8,128)(2,1)S(1)}, bf16[256,256]{1,0:T(8,128)(2,1)S(1)}, u32[]{:S(2)}, u32[]{:S(2)}) collective-permute-start(bf16[256,256]{1,0:T(8,128)(2,1)S(1)} %get-tuple-element.17), channel_id=1, source_target_pairs={{0,192},{8,200},{16,208},{24,216},{32,224},{40,232},{48,240},{56,2... | collective-permute-start | bytes 393224 | tf_op jit(solution)/shard_map/ppermute | solution.py:422
  5.8 6.3 %collective-permute-start.2 = (bf16[256,256]{1,0:T(8,128)(2,1)S(1)}, bf16[256,256]{1,0:T(8,128)(2,1)S(1)}, u32[]{:S(2)}, u32[]{:S(2)}) collective-permute-start(bf16[256,256]{1,0:T(8,128)(2,1)S(1)} %get-tuple-element.18), channel_id=1, source_target_pairs={{0,128},{8,136},{16,144},{24,152},{32,160},{40,168},{48,176},{56,1... | collective-permute-start | bytes 393224 | tf_op jit(solution)/shard_map/ppermute | solution.py:422
  12.1 27.3 %copy-start = (bf16[1024,256]{1,0:T(8,128)(2,1)S(1)}, bf16[1024,256]{1,0:T(8,128)(2,1)}, u32[]{:S(2)}) copy-start(bf16[1024,256]{1,0:T(8,128)(2,1)} %weight_ref.1) | copy-start | bytes 1572868

commit v3 on v2

--- a/solution.py
+++ b/solution.py
@@ -51,10 +51,10 @@
     y = lax.axis_index("seq") // NZ
     size = own_ref.shape[0]
     for k, ref in zip((0,) + Y_STEPS, (own_ref, to1_ref, to2_ref, to3_ref)):
-        first = pl.multiple_of(lax.rem(y + k, NY) * size, size)
+        first = pl.multiple_of((y ^ k) * size, size)
         ref[...] = jnp.dot(
             rows_ref[pl.ds(first, size), :], weight, preferred_element_type=jnp.float32
-        ).astype(jnp.bfloat16)
+        ).astype(ref.dtype)
 
 
 def project(rows, key_weight, value_weight):
@@ -63,7 +63,8 @@
         project_kernel,
         in_specs=[whole(pltpu.HBM)] * 3,
         out_specs=[whole()] * NY,
-        out_shape=[jax.ShapeDtypeStruct((tokens // NY, 2 * HD), jnp.bfloat16)] * NY,
+        out_shape=[jax.ShapeDtypeStruct((tokens // NY, 2 * HD), jnp.float32)]
+        + [jax.ShapeDtypeStruct((tokens // NY, 2 * HD), jnp.bfloat16)] * (NY - 1),
         scratch_shapes=[
             VMEM((tokens, features), jnp.bfloat16),
             VMEM((features, 2 * HD), jnp.bfloat16),
@@ -75,7 +76,7 @@
 
 
 def fold_kernel(after_ref, own_ref, from1_ref, from2_ref, from3_ref, out_ref):
-    total = own_ref[...].astype(jnp.float32)
+    total = own_ref[...]
     for ref in (from1_ref, from2_ref, from3_ref):
         total = total + ref[...].astype(jnp.float32)
     total = total.astype(jnp.bfloat16)
@@ -90,7 +91,7 @@
         fold_kernel,
         in_specs=[whole()] * 5,
         out_specs=whole(),
-        out_shape=jax.ShapeDtypeStruct(parts[0].shape, jnp.bfloat16),
+        out_shape=jax.ShapeDtypeStruct(parts[0].shape, parts[1].dtype),
         compiler_params=pltpu.CompilerParams(vmem_limit_bytes=8 * MIB),
         name="fold",
     )(after, *parts)
@@ -419,7 +420,7 @@
     own, *sent = project(prefill_rows, key_weight, value_weight)
     seq = [(y, z) for y in range(NY) for z in range(NZ)]
     came = [
-        lax.ppermute(part, "seq", [(y * NZ + z, (y + k) % NY * NZ + z) for y, z in seq])
+        lax.ppermute(part, "seq", [(y * NZ + z, (y ^ k) * NZ + z) for y, z in seq])
         for k, part in zip(Y_STEPS, sent)
     ]
     targets = span_target.T

time: 53.5 us -> 53.4 us (level)
  waiting for transfers between devices: 0.01 us -> 0.94 us
  blocking collectives: 39.2 us -> 38.6 us
    ppermute x3, waiting for transfers between devices: 0.01 us -> 0.94 us  [per_device(): lax.ppermute(part, 'seq', [(y * NZ + z, (y ^ k) * NZ + z) for y, z in seq])]
    all_to_all x1, blocking collectives: 13.6 us -> 12.9 us  [per_device(): lax.all_to_all(partial, 'seq', split_axis=0, concat_axis=0, tiled=True, a...]
  transfers between devices with their start and end apart: 3 -> 3, of which waited for: 0 -> 1; matrix products, arithmetic and copies ran while one was open for 0% -> 0% of each run, Pallas kernels for 9% -> 9%
where the time goes in v3:
time: 53.4 us; the launch traced here: 53.2 us
  blocking collectives  38.6 us (72%)
  Pallas kernels  8.07 us (15%)
  starting transfers between devices  4.84 us (9%)
  waiting for transfers between devices  0.94 us (2%)
  between operations  0.69 us (1%)
    all_to_all x1, blocking collectives, per_device(): lax.all_to_all(outgoing, 'seq', split_axis=0, concat_axis=0, tiled=True,...  13.1 us
    all_to_all x1, blocking collectives, per_device(): lax.all_to_all(partial, 'seq', split_axis=0, concat_axis=0, tiled=True, a...  12.9 us
    all_to_all x1, blocking collectives, per_device(): lax.all_to_all(shares, 'tp', split_axis=0, concat_axis=0, tiled=True, axi...  12.7 us
    ppermute x3, starting transfers between devices, per_device(): lax.ppermute(part, 'seq', [(y * NZ + z, (y ^ k) * NZ + z) for y, z in seq])  4.84 us
    pallas_call x1, Pallas kernels, cache_part(): pl.pallas_call(functools.partial(cache_kernel, requests, per_group), in_s...  4.73 us
    pallas_call x1, Pallas kernels, project(): pl.pallas_call(project_kernel, in_specs=[whole(pltpu.HBM)] * 3, out_specs...  1.45 us
  transfers between devices with their start and end apart: 3, of which 1 were waited for; matrix products, arithmetic and copies ran while one was open for 0% of the time, Pallas kernels for 9%

profile of v3, /device:TPU:1, one launch (start us, length us, event | category | flops | bytes accessed | tf_op | source)
XLA Modules:
  0.0 53.2 jit_solution(7480802353721620863)
XLA Ops:
  0.6 1.4 %project.1 = (f32[256,256]{1,0:T(8,128)S(1)}, bf16[256,256]{1,0:T(8,128)(2,1)S(1)}, bf16[256,256]{1,0:T(8,128)(2,1)S(1)}, bf16[256,256]{1,0:T(8,128)(2,1)S(1)}) custom-call(bf16[1024,256]{1,0:T(8,128)(2,1)} %rows_hbm.1, bf16[256,128]{1,0:T(8,128)(2,1)} %key_hbm.1, bf16[256,128]{1,0:T(8,128)(2,1)} %value_hbm.1), custom_call_target="tpu_custom_call" | custom-call | tf_op jit(solution)/shard_map/project/pallas_call | solution.py:62
  2.1 2.2 %collective-permute-start = (bf16[256,256]{1,0:T(8,128)(2,1)S(1)}, bf16[256,256]{1,0:T(8,128)(2,1)S(1)}, u32[]{:S(2)}, u32[]{:S(2)}) collective-permute-start(bf16[256,256]{1,0:T(8,128)(2,1)S(1)} %get-tuple-element.16), channel_id=1, source_target_pairs={{0,64},{8,72},{16,80},{24,88},{32,96},{40,104},{48,112},{56,120},{... | collective-permute-start | bytes 393224 | tf_op jit(solution)/shard_map/ppermute | solution.py:423
  4.3 1.9 %collective-permute-start.1 = (bf16[256,256]{1,0:T(8,128)(2,1)S(1)}, bf16[256,256]{1,0:T(8,128)(2,1)S(1)}, u32[]{:S(2)}, u32[]{:S(2)}) collective-permute-start(bf16[256,256]{1,0:T(8,128)(2,1)S(1)} %get-tuple-element.17), channel_id=1, source_target_pairs={{0,192},{8,200},{16,208},{24,216},{32,224},{40,232},{48,240},{56,2... | collective-permute-start | bytes 393224 | tf_op jit(solution)/shard_map/ppermute | solution.py:423
  6.2 0.7 %collective-permute-start.2 = (bf16[256,256]{1,0:T(8,128)(2,1)S(1)}, bf16[256,256]{1,0:T(8,128)(2,1)S(1)}, u32[]{:S(2)}, u32[]{:S(2)}) collective-permute-start(bf16[256,256]{1,0:T(8,128)(2,1)S(1)} %get-tuple-element.18), channel_id=1, source_target_pairs={{0,128},{8,136},{16,144},{24,152},{32,160},{40,168},{48,176},{56,1... | collective-permute-start | bytes 393224 | tf_op jit(solution)/shard_map/ppermute | solution.py:423
  6.9 4.7 %cache_part.1 = (f32[32,128]{1,0:T(8,128)S(1)}, f32[32,128]{1,0:T(8,128)S(1)}, f32[32,128]{1,0:T(8,128)S(1)}, bf16[256,32]{1,0:T(8,128)(2,1)S(1)}, bf16[256,32]{...) custom-call(s32[4]{0:T(128)} %len_hbm.1, bf16[4,1024]{1,0:T(4,128)(2,1)} %query_hbm.1, ...), custom_call_target="tpu_custom_call" | custom-call | flops 33554432 | bytes 4194304 | tf_op jit(solution)/shard_map/cache_part/pallas_call | solution.py:234
  11.7 0.0 copy-start
  11.7 0.0 collective-permute-done.from1_ref
  11.7 0.0 collective-permute-done.1.from2_ref
  11.7 0.9 %collective-permute-done.2.from3_ref = bf16[256,256]{1,0:T(8,128)(2,1)S(1)} collective-permute-done((bf16[256,256]{1,0:T(8,128)(2,1)S(1)}, bf16[256,256]{1,0:T(8,128)(2,1)S(1)}, u32[]{:S(2)}, u32[]{:S(2)}) %collective-permute-start.2) | collective-permute-done | bytes 131104 | tf_op jit(solution)/shard_map/ppermute | solution.py:423
  12.6 0.1 fold.1
  12.7 12.9 %all_to_all.15.parts_ref = bf16[8,32,256]{2,1,0:T(8,128)(2,1)S(1)} all-to-all(bf16[8,32,256]{2,1,0:T(8,128)(2,1)S(1)} %bitcast.3), channel_id=1, replica_groups={{56,24,40,8,48,16,32,0},{120,88,104,72,112,80,96,64},{184,152,168,136,1..., dimensions={0} | all-to-all | bytes 262144 | tf_op jit(solution)/shard_map/all_to_all | solution.py:433
  25.6 0.5 span_part.1
  26.1 13.1 %all_to_all.16.message_ref = bf16[32,40,128]{2,1,0:T(8,128)(2,1)S(1)} all-to-all(bf16[32,40,128]{2,1,0:T(8,128)(2,1)S(1)} %span_part.1), channel_id=1, replica_groups={{248,216,232,200,240,208,224,192,120,88,104,72,112,80,96,64,184,152,168..., dimensions={0} | all-to-all | bytes 655360 | tf_op jit(solution)/shard_map/all_to_all | solution.py:442
  39.2 0.0 copy-done
  39.2 0.7 %out_part.1 = f32[8,4,256]{2,1,0:T(4,128)S(1)} custom-call(bf16[32,40,128]{2,1,0:T(8,128)(2,1)S(1)} %all_to_all.16.message_ref, bf16[1024,256]{1,0:T(8,128)(2,1)S(1)} %copy-done), custom_call_target="tpu_custom_call" | custom-call | tf_op jit(solution)/shard_map/out_part/pallas_call | solution.py:353
  39.9 12.7 %all_to_all.17.share_ref = f32[8,4,256]{2,1,0:T(4,128)S(1)} all-to-all(f32[8,4,256]{2,1,0:T(4,128)S(1)} %out_part.1), channel_id=1, replica_groups={{7,6,5,4,3,2,1,0},{15,14,13,12,11,10,9,8},{23,22,21,20,19,18,17,16},{31..., dimensions={0} | all-to-all | bytes 65536 | tf_op jit(solution)/shard_map/all_to_all | solution.py:451
  52.5 0.7 %finish.1 = (bf16[4,256]{1,0:T(4,128)(2,1)}, bf16[64,128]{1,0:T(8,128)(2,1)}, bf16[64,128]{1,0:T(8,128)(2,1)}) custom-call(bf16[32,40,128]{2,1,0:T(8,128)(2,1)S(1)} %all_to_all.16.message_ref, f32[8,4,256]{2,1,0:T(4,128)S(1)} %all_to_all.17.share_ref), custom_call_target="tpu_custom_call" | custom-call | tf_op jit(solution)/shard_map/finish/pallas_call | solution.py:391
Async XLA Ops:
  2.1 9.6 %collective-permute-start = (bf16[256,256]{1,0:T(8,128)(2,1)S(1)}, bf16[256,256]{1,0:T(8,128)(2,1)S(1)}, u32[]{:S(2)}, u32[]{:S(2)}) collective-permute-start(bf16[256,256]{1,0:T(8,128)(2,1)S(1)} %get-tuple-element.16), channel_id=1, source_target_pairs={{0,64},{8,72},{16,80},{24,88},{32,96},{40,104},{48,112},{56,120},{... | collective-permute-start | bytes 393224 | tf_op jit(solution)/shard_map/ppermute | solution.py:423
  4.3 7.4 %collective-permute-start.1 = (bf16[256,256]{1,0:T(8,128)(2,1)S(1)}, bf16[256,256]{1,0:T(8,128)(2,1)S(1)}, u32[]{:S(2)}, u32[]{:S(2)}) collective-permute-start(bf16[256,256]{1,0:T(8,128)(2,1)S(1)} %get-tuple-element.17), channel_id=1, source_target_pairs={{0,192},{8,200},{16,208},{24,216},{32,224},{40,232},{48,240},{56,2... | collective-permute-start | bytes 393224 | tf_op jit(solution)/shard_map/ppermute | solution.py:423
  6.2 6.4 %collective-permute-start.2 = (bf16[256,256]{1,0:T(8,128)(2,1)S(1)}, bf16[256,256]{1,0:T(8,128)(2,1)S(1)}, u32[]{:S(2)}, u32[]{:S(2)}) collective-permute-start(bf16[256,256]{1,0:T(8,128)(2,1)S(1)} %get-tuple-element.18), channel_id=1, source_target_pairs={{0,128},{8,136},{16,144},{24,152},{32,160},{40,168},{48,176},{56,1... | collective-permute-start | bytes 393224 | tf_op jit(solution)/shard_map/ppermute | solution.py:423
  11.7 27.5 %copy-start = (bf16[1024,256]{1,0:T(8,128)(2,1)S(1)}, bf16[1024,256]{1,0:T(8,128)(2,1)}, u32[]{:S(2)}) copy-start(bf16[1024,256]{1,0:T(8,128)(2,1)} %weight_ref.1) | copy-start | bytes 1572868

commit v4 on v3

--- a/solution.py
+++ b/solution.py
@@ -454,7 +454,7 @@
         split_axis=0,
         concat_axis=0,
         tiled=True,
-        axis_index_groups=[list(reversed(range(tp_count)))],
+        axis_index_groups=[[listed(NY * NZ - NZ + place) for place in range(tp_count)]],
     )
     return finish(messages, shares)
 

time: 53.4 us -> 53.5 us (level)
  no operation moved by 1% of the time
where the time goes in v4:
time: 53.5 us; the launch traced here: 53.3 us
  blocking collectives  38.7 us (72%)
  Pallas kernels  8.07 us (15%)
  starting transfers between devices  4.84 us (9%)
  waiting for transfers between devices  0.94 us (2%)
  between operations  0.69 us (1%)
    all_to_all x1, blocking collectives, per_device(): lax.all_to_all(outgoing, 'seq', split_axis=0, concat_axis=0, tiled=True,...  13.1 us
    all_to_all x1, blocking collectives, per_device(): lax.all_to_all(partial, 'seq', split_axis=0, concat_axis=0, tiled=True, a...  12.9 us
    all_to_all x1, blocking collectives, per_device(): lax.all_to_all(shares, 'tp', split_axis=0, concat_axis=0, tiled=True, axi...  12.7 us
    ppermute x3, starting transfers between devices, per_device(): lax.ppermute(part, 'seq', [(y * NZ + z, (y ^ k) * NZ + z) for y, z in seq])  4.84 us
    pallas_call x1, Pallas kernels, cache_part(): pl.pallas_call(functools.partial(cache_kernel, requests, per_group), in_s...  4.73 us
    pallas_call x1, Pallas kernels, project(): pl.pallas_call(project_kernel, in_specs=[whole(pltpu.HBM)] * 3, out_specs...  1.45 us
  transfers between devices with their start and end apart: 3, of which 1 were waited for; matrix products, arithmetic and copies ran while one was open for 0% of the time, Pallas kernels for 9%

profile of v4, /device:TPU:1, one launch (start us, length us, event | category | flops | bytes accessed | tf_op | source)
XLA Modules:
  0.0 53.3 jit_solution(17766473515802607157)
XLA Ops:
  0.6 1.4 %project.1 = (f32[256,256]{1,0:T(8,128)S(1)}, bf16[256,256]{1,0:T(8,128)(2,1)S(1)}, bf16[256,256]{1,0:T(8,128)(2,1)S(1)}, bf16[256,256]{1,0:T(8,128)(2,1)S(1)}) custom-call(bf16[1024,256]{1,0:T(8,128)(2,1)} %rows_hbm.1, bf16[256,128]{1,0:T(8,128)(2,1)} %key_hbm.1, bf16[256,128]{1,0:T(8,128)(2,1)} %value_hbm.1), custom_call_target="tpu_custom_call" | custom-call | tf_op jit(solution)/shard_map/project/pallas_call | solution.py:62
  2.1 2.2 %collective-permute-start = (bf16[256,256]{1,0:T(8,128)(2,1)S(1)}, bf16[256,256]{1,0:T(8,128)(2,1)S(1)}, u32[]{:S(2)}, u32[]{:S(2)}) collective-permute-start(bf16[256,256]{1,0:T(8,128)(2,1)S(1)} %get-tuple-element.16), channel_id=1, source_target_pairs={{0,64},{8,72},{16,80},{24,88},{32,96},{40,104},{48,112},{56,120},{... | collective-permute-start | bytes 393224 | tf_op jit(solution)/shard_map/ppermute | solution.py:423
  4.3 1.9 %collective-permute-start.1 = (bf16[256,256]{1,0:T(8,128)(2,1)S(1)}, bf16[256,256]{1,0:T(8,128)(2,1)S(1)}, u32[]{:S(2)}, u32[]{:S(2)}) collective-permute-start(bf16[256,256]{1,0:T(8,128)(2,1)S(1)} %get-tuple-element.17), channel_id=1, source_target_pairs={{0,192},{8,200},{16,208},{24,216},{32,224},{40,232},{48,240},{56,2... | collective-permute-start | bytes 393224 | tf_op jit(solution)/shard_map/ppermute | solution.py:423
  6.2 0.7 %collective-permute-start.2 = (bf16[256,256]{1,0:T(8,128)(2,1)S(1)}, bf16[256,256]{1,0:T(8,128)(2,1)S(1)}, u32[]{:S(2)}, u32[]{:S(2)}) collective-permute-start(bf16[256,256]{1,0:T(8,128)(2,1)S(1)} %get-tuple-element.18), channel_id=1, source_target_pairs={{0,128},{8,136},{16,144},{24,152},{32,160},{40,168},{48,176},{56,1... | collective-permute-start | bytes 393224 | tf_op jit(solution)/shard_map/ppermute | solution.py:423
  6.9 4.7 %cache_part.1 = (f32[32,128]{1,0:T(8,128)S(1)}, f32[32,128]{1,0:T(8,128)S(1)}, f32[32,128]{1,0:T(8,128)S(1)}, bf16[256,32]{1,0:T(8,128)(2,1)S(1)}, bf16[256,32]{...) custom-call(s32[4]{0:T(128)} %len_hbm.1, bf16[4,1024]{1,0:T(4,128)(2,1)} %query_hbm.1, ...), custom_call_target="tpu_custom_call" | custom-call | flops 33554432 | bytes 4194304 | tf_op jit(solution)/shard_map/cache_part/pallas_call | solution.py:234
  11.7 0.0 copy-start
  11.7 0.0 collective-permute-done.from1_ref
  11.7 0.0 collective-permute-done.1.from2_ref
  11.7 0.9 %collective-permute-done.2.from3_ref = bf16[256,256]{1,0:T(8,128)(2,1)S(1)} collective-permute-done((bf16[256,256]{1,0:T(8,128)(2,1)S(1)}, bf16[256,256]{1,0:T(8,128)(2,1)S(1)}, u32[]{:S(2)}, u32[]{:S(2)}) %collective-permute-start.2) | collective-permute-done | bytes 131104 | tf_op jit(solution)/shard_map/ppermute | solution.py:423
  12.6 0.1 fold.1
  12.7 12.9 %all_to_all.15.parts_ref = bf16[8,32,256]{2,1,0:T(8,128)(2,1)S(1)} all-to-all(bf16[8,32,256]{2,1,0:T(8,128)(2,1)S(1)} %bitcast.3), channel_id=1, replica_groups={{56,24,40,8,48,16,32,0},{120,88,104,72,112,80,96,64},{184,152,168,136,1..., dimensions={0} | all-to-all | bytes 262144 | tf_op jit(solution)/shard_map/all_to_all | solution.py:433
  25.6 0.5 span_part.1
  26.1 13.1 %all_to_all.16.message_ref = bf16[32,40,128]{2,1,0:T(8,128)(2,1)S(1)} all-to-all(bf16[32,40,128]{2,1,0:T(8,128)(2,1)S(1)} %span_part.1), channel_id=1, replica_groups={{248,216,232,200,240,208,224,192,120,88,104,72,112,80,96,64,184,152,168..., dimensions={0} | all-to-all | bytes 655360 | tf_op jit(solution)/shard_map/all_to_all | solution.py:442
  39.2 0.0 copy-done
  39.2 0.7 %out_part.1 = f32[8,4,256]{2,1,0:T(4,128)S(1)} custom-call(bf16[32,40,128]{2,1,0:T(8,128)(2,1)S(1)} %all_to_all.16.message_ref, bf16[1024,256]{1,0:T(8,128)(2,1)S(1)} %copy-done), custom_call_target="tpu_custom_call" | custom-call | tf_op jit(solution)/shard_map/out_part/pallas_call | solution.py:353
  39.9 12.7 %all_to_all.17.share_ref = f32[8,4,256]{2,1,0:T(4,128)S(1)} all-to-all(f32[8,4,256]{2,1,0:T(4,128)S(1)} %out_part.1), channel_id=1, replica_groups={{7,3,5,1,6,2,4,0},{15,11,13,9,14,10,12,8},{23,19,21,17,22,18,20,16},{31..., dimensions={0} | all-to-all | bytes 65536 | tf_op jit(solution)/shard_map/all_to_all | solution.py:451
  52.6 0.7 %finish.1 = (bf16[4,256]{1,0:T(4,128)(2,1)}, bf16[64,128]{1,0:T(8,128)(2,1)}, bf16[64,128]{1,0:T(8,128)(2,1)}) custom-call(bf16[32,40,128]{2,1,0:T(8,128)(2,1)S(1)} %all_to_all.16.message_ref, f32[8,4,256]{2,1,0:T(4,128)S(1)} %all_to_all.17.share_ref), custom_call_target="tpu_custom_call" | custom-call | tf_op jit(solution)/shard_map/finish/pallas_call | solution.py:391
Async XLA Ops:
  2.1 9.6 %collective-permute-start = (bf16[256,256]{1,0:T(8,128)(2,1)S(1)}, bf16[256,256]{1,0:T(8,128)(2,1)S(1)}, u32[]{:S(2)}, u32[]{:S(2)}) collective-permute-start(bf16[256,256]{1,0:T(8,128)(2,1)S(1)} %get-tuple-element.16), channel_id=1, source_target_pairs={{0,64},{8,72},{16,80},{24,88},{32,96},{40,104},{48,112},{56,120},{... | collective-permute-start | bytes 393224 | tf_op jit(solution)/shard_map/ppermute | solution.py:423
  4.3 7.4 %collective-permute-start.1 = (bf16[256,256]{1,0:T(8,128)(2,1)S(1)}, bf16[256,256]{1,0:T(8,128)(2,1)S(1)}, u32[]{:S(2)}, u32[]{:S(2)}) collective-permute-start(bf16[256,256]{1,0:T(8,128)(2,1)S(1)} %get-tuple-element.17), channel_id=1, source_target_pairs={{0,192},{8,200},{16,208},{24,216},{32,224},{40,232},{48,240},{56,2... | collective-permute-start | bytes 393224 | tf_op jit(solution)/shard_map/ppermute | solution.py:423
  6.2 6.4 %collective-permute-start.2 = (bf16[256,256]{1,0:T(8,128)(2,1)S(1)}, bf16[256,256]{1,0:T(8,128)(2,1)S(1)}, u32[]{:S(2)}, u32[]{:S(2)}) collective-permute-start(bf16[256,256]{1,0:T(8,128)(2,1)S(1)} %get-tuple-element.18), channel_id=1, source_target_pairs={{0,128},{8,136},{16,144},{24,152},{32,160},{40,168},{48,176},{56,1... | collective-permute-start | bytes 393224 | tf_op jit(solution)/shard_map/ppermute | solution.py:423
  11.7 27.5 %copy-start = (bf16[1024,256]{1,0:T(8,128)(2,1)S(1)}, bf16[1024,256]{1,0:T(8,128)(2,1)}, u32[]{:S(2)}) copy-start(bf16[1024,256]{1,0:T(8,128)(2,1)} %weight_ref.1) | copy-start | bytes 1572868
